TPU v7x, 32 devices: a whole 2x2x4 slice. The times are simulated.
32 devices in a mesh: dp: 8 (over y, x, core), mp: 4 (over z).
Axes of the slice: x: 2, y: 2, z: 4, core: 2. Of those that a mesh axis runs over, the one named last changes fastest.
Arguments:
- tokens: bfloat16 [16384, 768], P('dp'), may hold values from -6 to 6
- cotangent: bfloat16 [16384, 768], P('dp'), may hold values from -6 to 6
- resets: int32 [32], P('dp'), may hold values from 0 to 1, as said below
- key_mask: int32 [16384], P('dp'), may hold values from 0 to 1, as said below
- truncation_segments: int32 [1], replicated, may hold values from 1 to 3
- qkv_weight: bfloat16 [3, 768, 768], P(None, 'dp', 'mp'), may hold values from -0.21875 to 0.21875
- out_weight: bfloat16 [768, 768], P('mp', 'dp'), may hold values from -1.5 to 1.5
- up_weight: bfloat16 [768, 3072], P('dp', 'mp'), may hold values from -0.21875 to 0.21875
- down_weight: bfloat16 [3072, 768], P('mp', 'dp'), may hold values from -0.109375 to 0.109375
- memory_init: bfloat16 [20, 768], P(None, 'dp'), may hold values from -6 to 6
- norm1_gain: bfloat16 [768], P('dp'), may hold values from 0.5 to 1.5
- first_norm_bias: bfloat16 [768], P('dp'), may hold values from -3 to 3
- norm2_gain: bfloat16 [768], P('dp'), may hold values from 0.5 to 1.5
- norm2_bias: bfloat16 [768], P('dp'), may hold values from -3 to 3
Outputs:
- layer_out: bfloat16 [16384, 768], P('dp')
- input_grad: float32 [16384, 768], P('dp', 'mp')
- qkv_grad: float32 [3, 768, 768], P(None, 'dp', 'mp')
- out_grad: float32 [768, 768], P('mp', 'dp')
- up_grad: float32 [768, 3072], P('dp', 'mp')
- down_grad: float32 [3072, 768], P('mp', 'dp')
- memory_init_gradient: float32 [20, 768], P(None, 'dp')
- norm1_gain_grad: float32 [768], P('dp')
- norm1_bias_grad: float32 [768], P('dp')
- norm2_gain_grad: float32 [768], P('dp')
- norm2_bias_grad: float32 [768], P('dp')
Inputs may be any that keep to these rules, and one draw needn't show every extreme that they name: `resets`: 1 marks a segment that starts a document; entries at multiples of 4 are 1, entries at odd indices and at indices 2 more than a multiple of 4 are 0, so every document spans two or more segments and the first of each aligned group four or more. `key_mask`: within each segment of 512 positions the ones come first; only a document's last segment (followed by a 1 in resets, or at the end of an aligned group of 4 segments) has zeros, and it keeps a one.
All inputs are finite; a program needn't handle non-finite values.
Results may differ from a plain program's by a relative error of at most 0.025.
Values may be sent and summed in bfloat16 or wider, within the bound.
A program may use at most 192 MiB of HBM per device.

v0:
```python
import jax
import jax.numpy as jnp
from jax import lax
from jax.sharding import PartitionSpec as P

HD = 64
SEG = 512
MEM = 20


EPSILON = 1e-05


def from_root(value, axis, source):
    kept = jnp.where(lax.axis_index(axis) == source, value, 0).astype(value.dtype)
    return lax.psum(kept, axis)


def normalize_rows(resid, gain, shift):
    center = resid - jnp.mean(resid, axis=-1, keepdims=True)
    inverse = lax.rsqrt(jnp.mean(center * center, axis=-1, keepdims=True) + EPSILON)
    normed = center * inverse
    return (normed * gain + shift, normed, inverse)


def normalize_back(grad_out, normed, inverse, gain):
    grad_hat = grad_out * gain
    grad_in = inverse * (
        grad_hat
        - jnp.mean(grad_hat, axis=-1, keepdims=True)
        - normed * jnp.mean(grad_hat * normed, axis=-1, keepdims=True)
    )
    return (grad_in, jnp.sum(grad_out * normed, axis=0), jnp.sum(grad_out, axis=0))


def gelu_slope(inner_act):
    cumulative = 0.5 * (1.0 + lax.erf(inner_act * 0.7071067811865476))
    density = jnp.exp(-0.5 * inner_act * inner_act) * 0.3989422804014327
    return cumulative + inner_act * density


def contract_rows(left, right):
    return jnp.einsum("ri,rj->ij", left, right, preferred_element_type=jnp.float32)


def times_transposed(left, right):
    return jnp.einsum("ri,ji->rj", left, right, preferred_element_type=jnp.float32)


def score_heads(queries, key_heads, valid_keys):
    scale = queries.shape[-1] ** (-0.5)
    scores = (
        jnp.einsum("qhd,khd->hqk", queries, key_heads, preferred_element_type=jnp.float32) * scale
    )
    return jnp.where(valid_keys[None, None, :] > 0, scores, -1e30)


def attend(queries, key_heads, value_heads, valid_keys):
    scores = score_heads(queries, key_heads, valid_keys)
    row_top = jnp.max(scores, axis=-1, keepdims=True)
    exp_total = jnp.sum(jnp.exp(scores - row_top), axis=-1, keepdims=True)
    logsum = row_top + jnp.log(exp_total)
    probs_low = jnp.exp(scores - logsum).astype(jnp.bfloat16)
    mixed_heads = jnp.einsum(
        "hqk,khd->qhd", probs_low, value_heads, preferred_element_type=jnp.float32
    )
    return (mixed_heads, logsum)


def attend_back(queries, key_heads, value_heads, valid_keys, logsum, grad_mixed):
    scale = queries.shape[-1] ** (-0.5)
    attn_probs = jnp.exp(score_heads(queries, key_heads, valid_keys) - logsum)
    probs_low = attn_probs.astype(jnp.bfloat16)
    grad_values = jnp.einsum(
        "hqk,qhd->khd", probs_low, grad_mixed, preferred_element_type=jnp.float32
    ).astype(jnp.bfloat16)
    grad_probs = jnp.einsum(
        "qhd,khd->hqk", grad_mixed, value_heads, preferred_element_type=jnp.float32
    )
    row_delta = jnp.sum(attn_probs * grad_probs, axis=-1, keepdims=True)
    grad_scores = (attn_probs * (grad_probs - row_delta)).astype(jnp.bfloat16)
    grad_queries = (
        scale
        * jnp.einsum("hqk,khd->qhd", grad_scores, key_heads, preferred_element_type=jnp.float32)
    ).astype(jnp.bfloat16)
    grad_keys = (
        scale * jnp.einsum("hqk,qhd->khd", grad_scores, queries, preferred_element_type=jnp.float32)
    ).astype(jnp.bfloat16)
    return (grad_queries, grad_keys, grad_values)


def share_sum(partial_value):
    return lax.psum_scatter(partial_value, "mp", scatter_dimension=0, tiled=True)


def rows_joined(share_low):
    return lax.all_gather(share_low, "mp", axis=0, tiled=True)


def shards(
    tokens,
    cotangent,
    resets,
    key_mask,
    truncation_segments,
    qkv_weight,
    out_weight,
    up_weight,
    down_weight,
    memory_init,
    norm1_gain,
    first_norm_bias,
    norm2_gain,
    norm2_bias,
):
    mp_size = lax.axis_size("mp")
    mp_index = lax.axis_index("mp")
    gathered = (
        lax.all_gather(qkv_weight, "dp", axis=1, tiled=True),
        lax.all_gather(out_weight, "dp", axis=1, tiled=True),
        lax.all_gather(up_weight, "dp", axis=0, tiled=True),
        lax.all_gather(down_weight, "dp", axis=1, tiled=True),
        lax.all_gather(memory_init, "dp", axis=1, tiled=True),
        lax.all_gather(norm1_gain, "dp", axis=0, tiled=True),
        lax.all_gather(first_norm_bias, "dp", axis=0, tiled=True),
        lax.all_gather(norm2_gain, "dp", axis=0, tiled=True),
        lax.all_gather(norm2_bias, "dp", axis=0, tiled=True),
    )
    attend_weights, output_weights, raise_weights, lower_weights = (
        gathered[0],
        gathered[1],
        gathered[2],
        gathered[3],
    )
    memory_start = gathered[4].astype(jnp.float32)
    gain_one = gathered[5].astype(jnp.float32)
    shift_one = gathered[6].astype(jnp.float32)
    gain_two = gathered[7].astype(jnp.float32)
    shift_two = gathered[8].astype(jnp.float32)
    model_width = tokens.shape[1]
    slot_count = resets.shape[0]
    row_total = SEG + MEM
    share_rows = row_total // mp_size
    first_row = mp_index * share_rows
    seg_index = jnp.arange(slot_count, dtype=jnp.int32)
    last_start = lax.cummax(jnp.where(resets > 0, seg_index, 0), axis=0)
    position = seg_index - last_start
    cut_flags = jnp.where((resets == 0) & (position % truncation_segments[0] == 0), 1, 0).astype(
        jnp.int32
    )

    def split_heads(projected):
        return (
            projected[0].reshape(row_total, -1, HD),
            projected[1].reshape(row_total, -1, HD),
            projected[2].reshape(row_total, -1, HD),
        )

    def forward_segment(memory, segment_item):
        token_block, reset_flag, block_mask = segment_item
        memory_in = jnp.where(reset_flag > 0, memory_start, memory)
        hidden = jnp.concatenate([memory_in, token_block.astype(jnp.float32)], axis=0)
        hidden_low = hidden.astype(jnp.bfloat16)
        valid_keys = jnp.concatenate([jnp.ones((MEM,), jnp.int32), block_mask], axis=0)
        projected = jnp.einsum(
            "rd,gdc->grc", hidden_low, attend_weights, preferred_element_type=jnp.float32
        ).astype(jnp.bfloat16)
        queries, key_heads, value_heads = split_heads(projected)
        mixed_heads, logsum = attend(queries, key_heads, value_heads, valid_keys)
        mixed_low = mixed_heads.reshape(row_total, -1).astype(jnp.bfloat16)
        attn_part = jnp.dot(mixed_low, output_weights, preferred_element_type=jnp.float32)
        hidden_mine = lax.dynamic_slice_in_dim(hidden, first_row, share_rows, 0)
        norm_mine, hat_one, inv_one = normalize_rows(
            hidden_mine + share_sum(attn_part), gain_one, shift_one
        )
        norm_low = rows_joined(norm_mine.astype(jnp.bfloat16))
        inner_act = jnp.dot(norm_low, raise_weights, preferred_element_type=jnp.float32)
        act_low = jax.nn.gelu(inner_act, approximate=False).astype(jnp.bfloat16)
        resid_two = norm_mine + share_sum(
            jnp.dot(act_low, lower_weights, preferred_element_type=jnp.float32)
        )
        final_mine, hat_two, inv_two = normalize_rows(resid_two, gain_two, shift_two)
        final_low = lax.all_gather(final_mine.astype(jnp.bfloat16), "mp", axis=0, tiled=True)
        next_memory = from_root(final_mine[:MEM].astype(jnp.bfloat16), "mp", 0).astype(jnp.float32)
        token_out = final_low[MEM:]
        kept_state = (
            hidden_low,
            projected,
            logsum,
            mixed_low,
            hat_one,
            inv_one,
            norm_low,
            inner_act,
            act_low,
            hat_two,
            inv_two,
            valid_keys,
        )
        return (next_memory, (token_out, kept_state))

    token_blocks = tokens.reshape(slot_count, SEG, model_width)
    mask_blocks = key_mask.reshape(slot_count, SEG)
    memory_zero = jnp.zeros((MEM, model_width), jnp.float32)
    _, (outputs_low, kept_all) = lax.scan(
        forward_segment, memory_zero, (token_blocks, resets, mask_blocks)
    )

    def backward_segment(carry_state, segment_item):
        grad_memory, grad_sums = carry_state
        kept_state, cot_block, reset_flag, cut_flag = segment_item
        (
            hidden_low,
            projected,
            logsum,
            mixed_low,
            hat_one,
            inv_one,
            norm_low,
            inner_act,
            act_low,
            hat_two,
            inv_two,
            valid_keys,
        ) = kept_state
        grad_final = jnp.concatenate([grad_memory, cot_block.astype(jnp.float32)], axis=0)
        grad_final_mine = lax.dynamic_slice_in_dim(grad_final, first_row, share_rows, 0)
        grad_two, gain_two_grad, shift_two_grad = normalize_back(
            grad_final_mine, hat_two, inv_two, gain_two
        )
        grad_two_low = rows_joined(grad_two.astype(jnp.bfloat16))
        lower_part = contract_rows(act_low, grad_two_low)
        grad_inner = (times_transposed(grad_two_low, lower_weights) * gelu_slope(inner_act)).astype(
            jnp.bfloat16
        )
        raise_part = contract_rows(norm_low, grad_inner)
        grad_norm = grad_two + share_sum(times_transposed(grad_inner, raise_weights))
        grad_one, gain_one_grad, shift_one_grad = normalize_back(
            grad_norm, hat_one, inv_one, gain_one
        )
        grad_attn_low = rows_joined(grad_one.astype(jnp.bfloat16))
        output_part = contract_rows(mixed_low, grad_attn_low)
        grad_mixed = (
            times_transposed(grad_attn_low, output_weights)
            .astype(jnp.bfloat16)
            .reshape(row_total, -1, HD)
        )
        queries, key_heads, value_heads = split_heads(projected)
        grad_queries, grad_keys, grad_values = attend_back(
            queries, key_heads, value_heads, valid_keys, logsum, grad_mixed
        )
        grad_proj = jnp.stack(
            [
                grad_queries.reshape(row_total, -1),
                grad_keys.reshape(row_total, -1),
                grad_values.reshape(row_total, -1),
            ],
            axis=0,
        )
        attend_part = jnp.einsum(
            "rd,grc->gdc", hidden_low, grad_proj, preferred_element_type=jnp.float32
        )
        back_part = jnp.einsum(
            "grc,gdc->rd", grad_proj, attend_weights, preferred_element_type=jnp.float32
        )
        summand = back_part + lax.dynamic_update_slice_in_dim(
            jnp.zeros_like(back_part), grad_one, first_row, 0
        )
        grad_cols = lax.psum_scatter(
            summand.astype(jnp.bfloat16), "mp", scatter_dimension=1, tiled=True
        ).astype(jnp.float32)
        grad_memory_in = lax.all_gather(grad_cols[:MEM], "mp", axis=1, tiled=True)
        dropped = (reset_flag > 0) | (cut_flag > 0)
        next_memory = jnp.where(dropped, jnp.zeros_like(grad_memory_in), grad_memory_in)
        memory_part = jnp.where(reset_flag > 0, grad_memory_in, jnp.zeros_like(grad_memory_in))
        additions = (
            attend_part,
            output_part,
            raise_part,
            lower_part,
            memory_part,
            gain_one_grad,
            shift_one_grad,
            gain_two_grad,
            shift_two_grad,
        )
        grad_sums = jax.tree.map(jnp.add, grad_sums, additions)
        return ((next_memory, grad_sums), grad_cols[MEM:])

    zero_gradient = (
        jnp.zeros(attend_weights.shape, jnp.float32),
        jnp.zeros(output_weights.shape, jnp.float32),
        jnp.zeros(raise_weights.shape, jnp.float32),
        jnp.zeros(lower_weights.shape, jnp.float32),
        jnp.zeros((MEM, model_width), jnp.float32),
        jnp.zeros((model_width,), jnp.float32),
        jnp.zeros((model_width,), jnp.float32),
        jnp.zeros((model_width,), jnp.float32),
        jnp.zeros((model_width,), jnp.float32),
    )
    cot_blocks = cotangent.reshape(slot_count, SEG, model_width)
    (_, grad_sums), input_cols = lax.scan(
        backward_segment,
        (memory_zero, zero_gradient),
        (kept_all, cot_blocks, resets, cut_flags),
        reverse=True,
    )
    norm_grads = (grad_sums[5], grad_sums[6], grad_sums[7], grad_sums[8])
    norm_grads = lax.psum((grad_sums[5], grad_sums[6], grad_sums[7], grad_sums[8]), "mp")
    reduced = (
        lax.psum_scatter(grad_sums[0], "dp", scatter_dimension=1, tiled=True),
        lax.psum_scatter(grad_sums[1], "dp", scatter_dimension=1, tiled=True),
        lax.psum_scatter(grad_sums[2], "dp", scatter_dimension=0, tiled=True),
        lax.psum_scatter(grad_sums[3], "dp", scatter_dimension=1, tiled=True),
        lax.psum_scatter(grad_sums[4], "dp", scatter_dimension=1, tiled=True),
        lax.psum_scatter(norm_grads[0], "dp", scatter_dimension=0, tiled=True),
        lax.psum_scatter(norm_grads[1], "dp", scatter_dimension=0, tiled=True),
        lax.psum_scatter(norm_grads[2], "dp", scatter_dimension=0, tiled=True),
        lax.psum_scatter(norm_grads[3], "dp", scatter_dimension=0, tiled=True),
    )
    layer_out = outputs_low.reshape(slot_count * SEG, model_width)
    input_grad = input_cols.reshape(slot_count * SEG, input_cols.shape[-1])
    return (
        layer_out,
        input_grad,
        reduced[0],
        reduced[1],
        reduced[2],
        reduced[3],
        reduced[4],
        reduced[5],
        reduced[6],
        reduced[7],
        reduced[8],
    )


def solution(mesh):
    return jax.shard_map(
        shards,
        mesh=mesh,
        in_specs=(
            P("dp", None),
            P("dp", None),
            P("dp"),
            P("dp"),
            P(),
            P(None, "dp", "mp"),
            P("mp", "dp"),
            P("dp", "mp"),
            P("mp", "dp"),
            P(None, "dp"),
            P("dp"),
            P("dp"),
            P("dp"),
            P("dp"),
        ),
        out_specs=(
            P("dp", None),
            P("dp", "mp"),
            P(None, "dp", "mp"),
            P("mp", "dp"),
            P("dp", "mp"),
            P("mp", "dp"),
            P(None, "dp"),
            P("dp"),
            P("dp"),
            P("dp"),
            P("dp"),
        ),
        check_vma=False,
    )
```

profile of v0, /device:TPU:0, one launch (start us, length us, event | category | flops | bytes accessed | tf_op | source)
XLA Modules:
  0.0 1465.8 jit_solution(16497260952465708148)
XLA Ops:
  70.0 602.3 %while.74 = (s32[]{:T(128)}, f32[20,768]{1,0:T(8,128)S(1)}, bf16[4,512,768]{2,1,0:T(8,128)(2,1)}, bf16[4,532,768]{2,1,0:T(8,128)(2,1)}, bf16[4,3,532,192]{2,3,1,...) while((s32[]{:T(128)}, f32[20,768]{1,0:T(8,128)S(1)}, ...), condition=%wide.region_10.11_spmd.clone, body=%wide.region_0.10_spmd.clone.sunk | while | flops 2144754560 | bytes 80302232 | solution.py:205
  83.3 36.7 %fusion.189 = f32[136,768]{1,0:T(8,128)S(1)} fusion(f32[532,768]{1,0:T(8,128)} %fusion.188), kind=kCustom, calls=%all-reduce-scatter.clone.1 | all-reduce-scatter fusion | flops 417793 | bytes 2052608 | tf_op jit(solution)/shard_map/while
  129.7 17.8 %all-gather.16 = bf16[4,133,768]{2,1,0:T(8,128)(2,1)S(1)} all-gather(bf16[1,133,768]{2,1,0:T(8,128)(2,1)S(1)} %fusion.191), channel_id=1, replica_groups=mesh['dp'=8,'mp'=4] {'mp'}, dimensions={0}, use_global_device_ids=true | all-gather | bytes 1021440 | tf_op jit(solution)/shard_map/while/body/eval_jaxpr/all_gather | solution.py:97
  157.9 31.4 %fusion.193 = f32[136,768]{1,0:T(8,128)S(1)} fusion(f32[532,768]{1,0:T(8,128)} %fusion.192), kind=kCustom, calls=%all-reduce-scatter.1.clone.1 | all-reduce-scatter fusion | flops 417793 | bytes 2052608 | tf_op jit(solution)/shard_map/while
  247.8 23.1 %fusion.189 = f32[136,768]{1,0:T(8,128)S(1)} fusion(f32[532,768]{1,0:T(8,128)} %fusion.188), kind=kCustom, calls=%all-reduce-scatter.clone.1 | all-reduce-scatter fusion | flops 417793 | bytes 2052608 | tf_op jit(solution)/shard_map/while
  307.3 25.4 %fusion.193 = f32[136,768]{1,0:T(8,128)S(1)} fusion(f32[532,768]{1,0:T(8,128)} %fusion.192), kind=kCustom, calls=%all-reduce-scatter.1.clone.1 | all-reduce-scatter fusion | flops 417793 | bytes 2052608 | tf_op jit(solution)/shard_map/while
  392.1 29.8 %fusion.189 = f32[136,768]{1,0:T(8,128)S(1)} fusion(f32[532,768]{1,0:T(8,128)} %fusion.188), kind=kCustom, calls=%all-reduce-scatter.clone.1 | all-reduce-scatter fusion | flops 417793 | bytes 2052608 | tf_op jit(solution)/shard_map/while
  431.8 18.9 %all-gather.16 = bf16[4,133,768]{2,1,0:T(8,128)(2,1)S(1)} all-gather(bf16[1,133,768]{2,1,0:T(8,128)(2,1)S(1)} %fusion.191), channel_id=1, replica_groups=mesh['dp'=8,'mp'=4] {'mp'}, dimensions={0}, use_global_device_ids=true | all-gather | bytes 1021440 | tf_op jit(solution)/shard_map/while/body/eval_jaxpr/all_gather | solution.py:97
  461.2 26.9 %fusion.193 = f32[136,768]{1,0:T(8,128)S(1)} fusion(f32[532,768]{1,0:T(8,128)} %fusion.192), kind=kCustom, calls=%all-reduce-scatter.1.clone.1 | all-reduce-scatter fusion | flops 417793 | bytes 2052608 | tf_op jit(solution)/shard_map/while
  513.1 17.7 %psum.48 = bf16[20,768]{1,0:T(8,128)(2,1)S(1)} all-reduce(bf16[20,768]{1,0:T(8,128)(2,1)S(1)} %slice_select_fusion.2), channel_id=1, replica_groups=mesh['dp'=8,'mp'=4] {'mp'}, use_global_device_ids=true, to_apply=%region_9.9 | all-reduce | flops 15360 | bytes 61440 | tf_op jit(solution)/shard_map/while/body/eval_jaxpr/psum | solution.py:16
  545.6 23.7 %fusion.189 = f32[136,768]{1,0:T(8,128)S(1)} fusion(f32[532,768]{1,0:T(8,128)} %fusion.188), kind=kCustom, calls=%all-reduce-scatter.clone.1 | all-reduce-scatter fusion | flops 417793 | bytes 2052608 | tf_op jit(solution)/shard_map/while
  605.5 22.9 %fusion.193 = f32[136,768]{1,0:T(8,128)S(1)} fusion(f32[532,768]{1,0:T(8,128)} %fusion.192), kind=kCustom, calls=%all-reduce-scatter.1.clone.1 | all-reduce-scatter fusion | flops 417793 | bytes 2052608 | tf_op jit(solution)/shard_map/while
  674.0 570.9 %while.75 = (s32[]{:T(128)}, f32[20,768]{1,0:T(8,128)S(1)}, f32[3,768,192]{1,2,0:T(8,128)}, f32[192,768]{1,0:T(8,128)}, f32[768,768]{1,0:T(8,128)}, /*index=5*/f...) while((s32[]{:T(128)}, f32[20,768]{1,0:T(8,128)S(1)}, ...), condition=%wide.region_24.25_spmd.clone, body=%wide.region_12.24_spmd.clone.sunk | while | flops 4336410624 | bytes 182487568 | solution.py:302
  678.8 18.8 %all-gather.18 = bf16[4,133,768]{2,1,0:T(8,128)(2,1)S(1)} all-gather(bf16[1,133,768]{2,1,0:T(8,128)(2,1)S(1)} %convert_bitcast_fusion.10), channel_id=1, replica_groups=mesh['dp'=8,'mp'=4] {'mp'}, dimensions={0}, use_global_device_ids=true | all-gather | bytes 1021440 | tf_op jit(solution)/shard_map/while/body/eval_jaxpr/all_gather | solution.py:97
  702.5 23.0 %fusion.224 = f32[136,768]{1,0:T(8,128)S(1)} fusion(f32[532,768]{1,0:T(8,128)S(1)} %fusion.223), kind=kCustom, calls=%all-reduce-scatter.2.clone.1 | all-reduce-scatter fusion | flops 417793 | bytes 2052608 | tf_op jit(solution)/shard_map/while
  816.1 17.5 %all-gather.18 = bf16[4,133,768]{2,1,0:T(8,128)(2,1)S(1)} all-gather(bf16[1,133,768]{2,1,0:T(8,128)(2,1)S(1)} %convert_bitcast_fusion.10), channel_id=1, replica_groups=mesh['dp'=8,'mp'=4] {'mp'}, dimensions={0}, use_global_device_ids=true | all-gather | bytes 1021440 | tf_op jit(solution)/shard_map/while/body/eval_jaxpr/all_gather | solution.py:97
  838.4 29.4 %fusion.224 = f32[136,768]{1,0:T(8,128)S(1)} fusion(f32[532,768]{1,0:T(8,128)S(1)} %fusion.223), kind=kCustom, calls=%all-reduce-scatter.2.clone.1 | all-reduce-scatter fusion | flops 417793 | bytes 2052608 | tf_op jit(solution)/shard_map/while
  983.0 29.5 %fusion.224 = f32[136,768]{1,0:T(8,128)S(1)} fusion(f32[532,768]{1,0:T(8,128)S(1)} %fusion.223), kind=kCustom, calls=%all-reduce-scatter.2.clone.1 | all-reduce-scatter fusion | flops 417793 | bytes 2052608 | tf_op jit(solution)/shard_map/while
  1126.9 30.2 %fusion.224 = f32[136,768]{1,0:T(8,128)S(1)} fusion(f32[532,768]{1,0:T(8,128)S(1)} %fusion.223), kind=kCustom, calls=%all-reduce-scatter.2.clone.1 | all-reduce-scatter fusion | flops 417793 | bytes 2052608 | tf_op jit(solution)/shard_map/while
  1256.4 22.3 %all-reduce.15 = (f32[768]{0:T(1024)S(1)}, f32[768]{0:T(1024)S(1)}, f32[768]{0:T(1024)S(1)}, f32[768]{0:T(1024)S(1)}) all-reduce(f32[768]{0:T(1024)S(1)} %copy-done.41, f32[768]{0:T(1024)S(1)} %copy-done.44, f32[768]{0:T(1024)S(1)} %copy-done.47, f32[768]{0:T(1024)S(1)} %copy-done.50), channel_id=11, replica_groups=mesh['dp'=8,'mp'=4] {'dp'}, use_global_device_ids=true, to_apply=%region_31.32.clone | all-reduce | flops 3072 | bytes 24576
  1291.9 27.4 %reduce-scatter.27.cloned.1.call-done = f32[96,192]{1,0:T(8,128)} async-done(((f32[768,192]{1,0:T(8,128)}), f32[96,192]{1,0:T(8,128)}) %reduce-scatter.27.cloned.1.call-update) | async-done | bytes 73744
  1321.0 44.8 %reduce-scatter.21.cloned.1.call-done = f32[3,96,192]{2,1,0:T(8,128)} async-done(((f32[3,768,192]{2,1,0:T(8,128)}), f32[3,96,192]{2,1,0:T(8,128)}) %reduce-scatter.21.cloned.1.call-update) | async-done | bytes 221200 | tf_op jit(solution)/shard_map/reduce_scatter | solution.py:311
  1365.8 46.6 %reduce-scatter.25.cloned.1.call-done = f32[768,96]{0,1:T(8,128)} async-done(((f32[768,768]{0,1:T(8,128)}), f32[768,96]{0,1:T(8,128)}) %reduce-scatter.25.cloned.1.call-update) | async-done | bytes 294928 | tf_op jit(solution)/shard_map/reduce_scatter | solution.py:314
  1412.4 46.4 %reduce-scatter.23.cloned.1.call-done = f32[96,768]{1,0:T(8,128)} async-done(((f32[768,768]{1,0:T(8,128)}), f32[96,768]{1,0:T(8,128)}) %reduce-scatter.23.cloned.1.call-update) | async-done | bytes 294928 | tf_op jit(solution)/shard_map/reduce_scatter | solution.py:313
  (955 shorter events, 821.3 us)
Async XLA Ops:
  7.2 60.5 %all-gather.26.cloned.1.call-start = ((), (), s32[]{:S(2)}) async-start(), calls=%async_computation.7 | async-start | bytes 1327104 | tf_op jit(solution)/shard_map/all_gather | solution.py:122
  7.9 62.1 %all-gather.24.cloned.1.call-start = ((), (), s32[]{:S(2)}) async-start(), calls=%async_computation.6 | async-start | bytes 1327104 | tf_op jit(solution)/shard_map/all_gather | solution.py:121
  120.7 7.3 collective-permute-start
  189.3 7.4 collective-permute-start.1
  271.6 7.9 collective-permute-start
  332.7 9.4 collective-permute-start.1
  422.6 7.6 collective-permute-start
  488.1 6.8 collective-permute-start.1
  570.0 7.5 collective-permute-start
  628.5 6.9 collective-permute-start.1
  674.2 121.6 %reduce-scatter.31.cloned.1.call-start = ((), (), s32[]{:S(2)}) async-start(), calls=%async_computation.13 | async-start | bytes 1228800 | tf_op jit(solution)/shard_map/while
  725.6 9.1 collective-permute-start.2
  811.5 129.0 %reduce-scatter.31.cloned.1.call-start = ((), (), s32[]{:S(2)}) async-start(), calls=%async_computation.13 | async-start | bytes 1228800 | tf_op jit(solution)/shard_map/while
  867.8 9.7 collective-permute-start.2
  956.2 128.1 %reduce-scatter.31.cloned.1.call-start = ((), (), s32[]{:S(2)}) async-start(), calls=%async_computation.13 | async-start | bytes 1228800 | tf_op jit(solution)/shard_map/while
  1012.5 9.7 collective-permute-start.2
  1099.9 129.0 %reduce-scatter.31.cloned.1.call-start = ((), (), s32[]{:S(2)}) async-start(), calls=%async_computation.13 | async-start | bytes 1228800 | tf_op jit(solution)/shard_map/while
  1157.1 9.7 collective-permute-start.2
  1166.8 24.9 %copy-start.33 = (pred[532]{0:T(1024)(128)(4,1)}, pred[532]{0:T(1024)(128)(4,1)S(1)}, u32[]{:S(2)}) copy-start(pred[532]{0:T(1024)(128)(4,1)S(1)} %compare_reduce_fusion.2) | copy-start | bytes 1600 | tf_op jit(solution)/shard_map/while
  1244.9 45.5 %reduce-scatter.29.cloned.1.call-start = ((), (), s32[]{:S(2)}) async-start(), calls=%async_computation.12 | async-start | bytes 442368
  1245.9 73.4 %reduce-scatter.27.cloned.1.call-start = ((), (), s32[]{:S(2)}) async-start(), calls=%async_computation.11 | async-start | bytes 884736
  1248.2 117.6 %reduce-scatter.21.cloned.1.call-start = ((), (), s32[]{:S(2)}) async-start(), calls=%async_computation.8 | async-start | bytes 2654208 | tf_op jit(solution)/shard_map/reduce_scatter | solution.py:311
  1251.3 161.2 %reduce-scatter.25.cloned.1.call-start = ((), (), s32[]{:S(2)}) async-start(), calls=%async_computation.10 | async-start | bytes 2654208 | tf_op jit(solution)/shard_map/reduce_scatter | solution.py:314
  1254.9 203.9 %reduce-scatter.23.cloned.1.call-start = ((), (), s32[]{:S(2)}) async-start(), calls=%async_computation.9 | async-start | bytes 2654208 | tf_op jit(solution)/shard_map/reduce_scatter | solution.py:313
  (210 other events, 1224.3 us)
Sparse Core Ops, SparseCore 0:
  9.9 28.2 all-gather.25
  40.1 25.2 all-gather.23
  771.5 24.2 reduce-scatter.30
  914.3 26.1 reduce-scatter.30
  1059.1 25.1 reduce-scatter.30
  1204.0 24.8 reduce-scatter.30
  1248.8 32.3 reduce-scatter.28
  1284.3 34.9 reduce-scatter.26
  1323.3 42.4 reduce-scatter.20
  1369.9 42.4 reduce-scatter.24
  1416.4 42.4 reduce-scatter.22
where the time goes:
time: 1480 us; the launch traced here: 1470 us
  blocking collectives  801 us (54%)
  waiting for transfers between devices  201 us (14%)
  matrix products  169 us (11%)
  local copies, waits for them, and re-layouts  146 us (10%)
  other arithmetic  87.4 us (6%)
  starting transfers between devices  27.1 us (2%)
  loops' own time  17.4 us (1%)
  between operations  16.6 us (1%)
    while x12, blocking collectives  332 us
    all_gather x12, blocking collectives, rows_joined(): return lax.all_gather(share_low, 'mp', axis=0, tiled=True)  203 us
    psum x4, blocking collectives, from_root(): return lax.psum(kept, axis)  69.1 us
    all_gather x4, blocking collectives, forward_segment(): lax.all_gather(final_mine.astype(jnp.bfloat16), 'mp', axis=0, tiled=True)  64.7 us
    all_gather x4, blocking collectives, backward_segment(): grad_memory_in = lax.all_gather(grad_cols[:MEM], 'mp', axis=1, tiled=True)  53.1 us
    reduce_scatter x1, waiting for transfers between devices, shards(): lax.psum_scatter(grad_sums[3], 'dp', scatter_dimension=1, tiled=True)  46.6 us
    reduce_scatter x1, waiting for transfers between devices, shards(): lax.psum_scatter(grad_sums[2], 'dp', scatter_dimension=0, tiled=True)  46.4 us
    while x460, local copies, waits for them, and re-layouts  45.2 us
  transfers between devices with their start and end apart: 23, of which 8 were waited for; matrix products, arithmetic and copies ran while one was open for 10% of the time, Pallas kernels for 0%

commit v1 on v0

v1 whole, which is shorter than its diff:
```python
import functools

import jax
import jax.numpy as jnp
from jax import lax
from jax.experimental import pallas as pl
from jax.experimental.pallas import tpu as pltpu
from jax.sharding import PartitionSpec as P

HD = 64
SEG = 512
MEM = 20
PAD = 32
ROWS = SEG + PAD
EPSILON = 1e-05
MESH = pl.DeviceIdType.MESH
F32 = jnp.float32
BF16 = jnp.bfloat16


def nn(a, b):
    return lax.dot_general(a, b, (((1,), (0,)), ((), ())), preferred_element_type=F32)


def nt(a, b):
    return lax.dot_general(a, b, (((1,), (1,)), ((), ())), preferred_element_type=F32)


def tn(a, b):
    return lax.dot_general(a, b, (((0,), (0,)), ((), ())), preferred_element_type=F32)


def normalize(resid):
    center = resid - jnp.mean(resid, axis=-1, keepdims=True)
    inverse = lax.rsqrt(jnp.mean(center * center, axis=-1, keepdims=True) + EPSILON)
    return center * inverse, inverse


def normalize_back(grad_out, hat, inverse, gain):
    grad_hat = grad_out * gain
    return inverse * (
        grad_hat
        - jnp.mean(grad_hat, axis=-1, keepdims=True)
        - hat * jnp.mean(grad_hat * hat, axis=-1, keepdims=True)
    )


def layer_kernel(
    n,
    tok_hbm, cot_hbm, flags, kbias, norms, mem_init, wqkv_hbm, wot_hbm, wup_hbm, wdnt_hbm,
    lo_hbm, dx_hbm, dqkv_hbm, dot_hbm, dup_hbm, ddnt_hbm, dmem, dnorm,
    wqkv, wot, wup, wdnt, hid, cot, qkv, probs, mixed, hat1, inv1, nlow, act, slope, hat2, inv2, lout,
    g2low, ginner, gone, g1low, gmix, dk32, dv32, dqkv, dxs,
    mem_recv, mem_send, gm_recv, gm_send,
    load_sem, w_sem, lo_sem, dx_sem, lo_send, lo_recv, dx_send, dx_recv, chain_sem,
):
    dp = lax.axis_index("dp")
    mp = lax.axis_index("mp")
    width = hid.shape[1]
    pairs = width // 128
    parts = wup.shape[0]
    tok_rows = pl.ds(0, SEG)
    mem_rows = pl.ds(SEG, PAD)

    load_tok = pltpu.make_async_copy(
        tok_hbm.at[pl.ds(mp * SEG, SEG)], hid.at[tok_rows], load_sem.at[0]
    )
    load_cot = pltpu.make_async_copy(cot_hbm.at[pl.ds(mp * SEG, SEG)], cot, load_sem.at[1])
    load_tok.start()
    loads = [
        pltpu.make_async_copy(src, dst, w_sem.at[i])
        for i, (src, dst) in enumerate(
            ((wqkv_hbm, wqkv), (wot_hbm, wot), (wup_hbm, wup), (wdnt_hbm, wdnt))
        )
    ]
    for load in loads:
        load.start()
    load_cot.start()

    @pl.when(mp == 0)
    def _():
        mem_recv[...] = jnp.zeros_like(mem_recv)

    @pl.when(mp == n - 1)
    def _():
        gm_recv[...] = jnp.zeros_like(gm_recv)

    barrier = pltpu.get_barrier_semaphore()
    for step in range(1, n):
        pl.semaphore_signal(
            barrier, inc=1, device_id=(dp, lax.rem(mp + step, n)), device_id_type=MESH
        )
    pl.semaphore_wait(barrier, n - 1)

    gain1, bias1 = norms[0:1], norms[1:2]
    gain2, bias2 = norms[2:3], norms[3:4]
    lane = lax.broadcasted_iota(jnp.int32, (1, 128), 1)
    half_scaled = [
        jnp.where(lane < HD, HD**-0.5, 0.0).astype(BF16),
        jnp.where(lane < HD, 0.0, HD**-0.5).astype(BF16),
    ]
    half_one = [
        jnp.where(lane < HD, 1.0, 0.0).astype(BF16),
        jnp.where(lane < HD, 0.0, 1.0).astype(BF16),
    ]

    def project(rows):
        x = hid[rows, :]
        for g in range(3):
            qkv[g, rows, :] = nn(x, wqkv[g]).astype(BF16)

    def attend(rows, count):
        @pl.loop(0, pairs)
        def _(pair):
            lanes = pl.ds(pl.multiple_of(pair * 128, 128), 128)
            q = qkv[0, rows, lanes]
            k = qkv[1, :, lanes]
            v = qkv[2, :, lanes]
            outs = []
            for half in range(2):
                scores = nt(q * half_scaled[half], k) + kbias[...]
                top = jnp.max(scores, axis=-1, keepdims=True)
                e = jnp.exp(scores - top)
                p = (e * (1.0 / jnp.sum(e, axis=-1, keepdims=True))).astype(BF16)
                probs[2 * pair + half, rows, :] = p
                outs.append(nn(p, v))
            first = lax.broadcasted_iota(jnp.int32, (count, 128), 1) < HD
            mixed[rows, lanes] = jnp.where(first, outs[0], outs[1]).astype(BF16)

    def feed(rows):
        resid = hid[rows, :].astype(F32) + nt(mixed[rows, :], wot[...])
        h1, i1 = normalize(resid)
        hat1[rows, :] = h1
        inv1[rows, :] = i1
        norm_one = h1 * gain1 + bias1
        nlow[rows, :] = norm_one.astype(BF16)
        hat2[rows, :] = norm_one

        @pl.loop(0, parts)
        def _(j):
            inner = nn(nlow[rows, :], wup[j])
            cumulative = 0.5 * (1.0 + lax.erf(inner * 0.7071067811865476))
            density = jnp.exp(-0.5 * inner * inner) * 0.3989422804014327
            a = (inner * cumulative).astype(BF16)
            act[j, rows, :] = a
            slope[j, rows, :] = (cumulative + inner * density).astype(BF16)
            hat2[rows, :] += nt(a, wdnt[j])

        h2, i2 = normalize(hat2[rows, :])
        hat2[rows, :] = h2
        inv2[rows, :] = i2
        return (h2 * gain2 + bias2).astype(BF16)

    def feed_back(rows, grad_final):
        h2 = hat2[rows, :]
        dnorm[2:3, :] += jnp.sum(grad_final * h2, axis=0, keepdims=True)
        dnorm[3:4, :] += jnp.sum(grad_final, axis=0, keepdims=True)
        g2 = normalize_back(grad_final, h2, inv2[rows, :], gain2)
        g2low[rows, :] = g2.astype(BF16)
        gone[rows, :] = g2

        @pl.loop(0, parts)
        def _(j):
            gi = (nn(g2low[rows, :], wdnt[j]) * slope[j, rows, :].astype(F32)).astype(BF16)
            ginner[j, rows, :] = gi
            gone[rows, :] += nt(gi, wup[j])

        grad_norm = gone[rows, :]
        h1 = hat1[rows, :]
        dnorm[0:1, :] += jnp.sum(grad_norm * h1, axis=0, keepdims=True)
        dnorm[1:2, :] += jnp.sum(grad_norm, axis=0, keepdims=True)
        g1 = normalize_back(grad_norm, h1, inv1[rows, :], gain1)
        gone[rows, :] = g1
        low = g1.astype(BF16)
        g1low[rows, :] = low
        gmix[rows, :] = nn(low, wot[...]).astype(BF16)

    def attend_back(rows, count, first_time):
        @pl.loop(0, pairs)
        def _(pair):
            lanes = pl.ds(pl.multiple_of(pair * 128, 128), 128)
            q = qkv[0, rows, lanes]
            k = qkv[1, :, lanes]
            v = qkv[2, :, lanes]
            g = gmix[rows, lanes]
            dqs = []
            dk = None
            dv = None
            for half in range(2):
                p = probs[2 * pair + half, rows, :]
                gh = g * half_one[half]
                dprob = nt(gh, v)
                pf = p.astype(F32)
                delta = jnp.sum(pf * dprob, axis=-1, keepdims=True)
                ds = (pf * (dprob - delta)).astype(BF16)
                dv_h = tn(p, gh)
                dk_h = tn(ds, q * half_scaled[half])
                dqs.append(nn(ds, k))
                dk = dk_h if dk is None else dk + dk_h
                dv = dv_h if dv is None else dv + dv_h
            first = lax.broadcasted_iota(jnp.int32, (count, 128), 1) < HD
            dqkv[0, rows, lanes] = (jnp.where(first, dqs[0], dqs[1]) * HD**-0.5).astype(BF16)
            if first_time:
                dk32[:, lanes] = dk
                dv32[:, lanes] = dv
            else:
                dk32[:, lanes] += dk
                dv32[:, lanes] += dv

    def chain_copy(src, dst, slot, peer):
        return pltpu.make_async_remote_copy(
            src_ref=src, dst_ref=dst,
            send_sem=chain_sem.at[2 * slot], recv_sem=chain_sem.at[2 * slot + 1],
            device_id=(dp, peer), device_id_type=MESH,
        )

    forward_copy = chain_copy(mem_send, mem_recv, 0, lax.rem(mp + 1, n))
    backward_copy = chain_copy(gm_send, gm_recv, 1, lax.rem(mp + n - 1, n))

    load_tok.wait()
    loads[0].wait()

    @pl.loop(0, 2)
    def _(c):
        project(pl.ds(pl.multiple_of(c * 256, 256), 256))

    @pl.when(mp > 0)
    def _():
        forward_copy.wait_recv()

    hid[mem_rows, :] = jnp.where(
        flags[0:1, 0:1] > 0, mem_init[...].astype(F32), mem_recv[...].astype(F32)
    ).astype(BF16)
    project(mem_rows)
    attend(mem_rows, PAD)
    for load in loads[1:]:
        load.wait()
    mem_send[...] = feed(mem_rows)

    @pl.when(mp < n - 1)
    def _():
        forward_copy.start()

    attend(tok_rows, SEG)

    @pl.loop(0, 2)
    def _(c):
        rows = pl.ds(pl.multiple_of(c * 256, 256), 256)
        lout[rows, :] = feed(rows)

    own = pl.ds(mp * SEG, SEG)
    keep_out = pltpu.make_async_copy(lout, lo_hbm.at[own], lo_sem)
    keep_out.start()
    out_copies = []
    for step in range(1, n):
        copy = pltpu.make_async_remote_copy(
            src_ref=lout, dst_ref=lo_hbm.at[own],
            send_sem=lo_send.at[step - 1], recv_sem=lo_recv.at[step - 1],
            device_id=(dp, lax.rem(mp + step, n)), device_id_type=MESH,
        )
        copy.start()
        out_copies.append(copy)

    dnorm[...] = jnp.zeros_like(dnorm)
    load_cot.wait()

    @pl.loop(0, 2)
    def _(c):
        rows = pl.ds(pl.multiple_of(c * 256, 256), 256)
        feed_back(rows, cot[rows, :].astype(F32))

    attend_back(tok_rows, SEG, True)

    @pl.when(mp < n - 1)
    def _():
        backward_copy.wait_recv()

    feed_back(mem_rows, gm_recv[...].astype(F32))
    attend_back(mem_rows, PAD, False)

    def input_grad(rows):
        return (
            gone[rows, :]
            + nt(dqkv[0, rows, :], wqkv[0])
            + nt(dqkv[1, rows, :], wqkv[1])
            + nt(dqkv[2, rows, :], wqkv[2])
        )

    dqkv[1, :, :] = dk32[...].astype(BF16)
    dqkv[2, :, :] = dv32[...].astype(BF16)
    gmem = input_grad(mem_rows)
    gm_send[...] = jnp.where(flags[1:2, 0:1] > 0, gmem, 0.0).astype(BF16)

    @pl.when(mp > 0)
    def _():
        backward_copy.start()

    dmem[...] = jnp.where(flags[0:1, 0:1] > 0, gmem, 0.0)

    cols = width // n

    @pl.loop(0, 2)
    def _(c):
        rows = pl.ds(pl.multiple_of(c * 256, 256), 256)
        g = input_grad(rows).astype(BF16)
        for j in range(n):
            dxs[j, rows, :] = g[:, j * cols : (j + 1) * cols]

    keep_dx = pltpu.make_async_copy(dxs.at[mp], dx_hbm.at[mp], dx_sem)
    keep_dx.start()
    dx_copies = []
    for step in range(1, n):
        peer = lax.rem(mp + step, n)
        copy = pltpu.make_async_remote_copy(
            src_ref=dxs.at[peer], dst_ref=dx_hbm.at[mp],
            send_sem=dx_send.at[step - 1], recv_sem=dx_recv.at[step - 1],
            device_id=(dp, peer), device_id_type=MESH,
        )
        copy.start()
        dx_copies.append(copy)

    @pl.loop(0, parts)
    def _(j):
        wdnt[j] = tn(g2low[...], act[j]).astype(BF16)

    @pl.loop(0, parts)
    def _(j):
        wup[j] = tn(nlow[...], ginner[j]).astype(BF16)

    wot[...] = tn(g1low[...], mixed[...]).astype(BF16)

    @pl.loop(0, 3)
    def _(g):
        wqkv[g] = tn(hid[...], dqkv[g]).astype(BF16)

    stores = [
        pltpu.make_async_copy(src, dst, w_sem.at[i])
        for i, (src, dst) in enumerate(
            ((wqkv, dqkv_hbm), (wot, dot_hbm), (wup, dup_hbm), (wdnt, ddnt_hbm))
        )
    ]
    for store in stores:
        store.start()
    for store in stores:
        store.wait()
    keep_out.wait()
    keep_dx.wait()
    for copy in out_copies + dx_copies:
        copy.wait()

    @pl.when(mp < n - 1)
    def _():
        forward_copy.wait_send()

    @pl.when(mp > 0)
    def _():
        backward_copy.wait_send()


def run_layer(n, tokens, cotangent, flags, kbias, norms, mem_init, wqkv, wot, wup, wdnt):
    width = tokens.shape[1]
    parts = wup.shape[0]
    heads = width // HD
    vmem = pl.BlockSpec(memory_space=pltpu.VMEM)
    anyspace = pl.BlockSpec(memory_space=pl.ANY)
    out_shape = (
        jax.ShapeDtypeStruct((n * SEG, width), BF16),
        jax.ShapeDtypeStruct((n, SEG, width // n), BF16),
        jax.ShapeDtypeStruct(wqkv.shape, BF16),
        jax.ShapeDtypeStruct(wot.shape, BF16),
        jax.ShapeDtypeStruct(wup.shape, BF16),
        jax.ShapeDtypeStruct(wdnt.shape, BF16),
        jax.ShapeDtypeStruct((PAD, width), F32),
        jax.ShapeDtypeStruct((8, width), F32),
    )
    row_bf = pltpu.VMEM((ROWS, width), BF16)
    row_f = pltpu.VMEM((ROWS, width), F32)
    one_f = pltpu.VMEM((ROWS, 1), F32)
    wide = pltpu.VMEM((parts, ROWS, width), BF16)
    mem_bf = pltpu.VMEM((PAD, width), BF16)
    sems = pltpu.SemaphoreType.DMA
    return pl.pallas_call(
        functools.partial(layer_kernel, n),
        out_shape=out_shape,
        in_specs=[anyspace] * 2 + [vmem] * 4 + [anyspace] * 4,
        out_specs=(anyspace,) * 6 + (vmem,) * 2,
        scratch_shapes=[
            pltpu.VMEM(wqkv.shape, BF16), pltpu.VMEM(wot.shape, BF16),
            pltpu.VMEM(wup.shape, BF16), pltpu.VMEM(wdnt.shape, BF16),
            row_bf, pltpu.VMEM((SEG, width), BF16), pltpu.VMEM((3, ROWS, width), BF16),
            pltpu.VMEM((heads, ROWS, ROWS), BF16), row_bf, row_f, one_f, row_bf, wide, wide, row_f,
            one_f, pltpu.VMEM((SEG, width), BF16),
            row_bf, wide, row_f, row_bf, row_bf, row_f, row_f, pltpu.VMEM((3, ROWS, width), BF16),
            pltpu.VMEM((n, SEG, width // n), BF16),
            mem_bf, mem_bf, mem_bf, mem_bf,
            sems((2,)), sems((4,)), sems, sems, sems((n - 1,)), sems((n - 1,)), sems((n - 1,)), sems((n - 1,)),
            sems((4,)),
        ],
        compiler_params=pltpu.CompilerParams(
            collective_id=0, has_side_effects=True, vmem_limit_bytes=62 * 2**20
        ),
        cost_estimate=pl.CostEstimate(
            flops=26_000_000_000, bytes_accessed=40_000_000, transcendentals=10_000_000
        ),
    )(tokens, cotangent, flags, kbias, norms, mem_init, wqkv, wot, wup, wdnt)


def shards(
    tokens, cotangent, resets, key_mask, truncation_segments, qkv_weight, out_weight, up_weight,
    down_weight, memory_init, norm1_gain, first_norm_bias, norm2_gain, norm2_bias,
):
    n = lax.axis_size("mp")
    m = lax.axis_size("dp")
    mp = lax.axis_index("mp")
    dp = lax.axis_index("dp")
    width = tokens.shape[1]
    slots = resets.shape[0]
    rows = width // m
    cols = width // n
    block = jnp.concatenate([qkv_weight, out_weight.T[None]], axis=0)
    block = lax.all_gather(block, ("mp", "dp"), axis=0)
    block = block.reshape(n, m, 4, rows, cols).transpose(2, 1, 3, 0, 4).reshape(4, width, width)
    wup = lax.all_gather(up_weight, ("mp", "dp"), axis=0).reshape(n, width, -1)
    wdnt = lax.all_gather(down_weight.T, ("mp", "dp"), axis=0).reshape(n, width, -1)
    small = jnp.concatenate(
        [norm1_gain[None], first_norm_bias[None], norm2_gain[None], norm2_bias[None], memory_init],
        axis=0,
    )
    small = lax.all_gather(small, "dp", axis=1, tiled=True)
    norms = jnp.pad(small[:4].astype(F32), ((0, 4), (0, 0)))
    mem_init = jnp.pad(small[4:], ((0, PAD - MEM), (0, 0)))
    seg_index = jnp.arange(slots, dtype=jnp.int32)
    last_start = lax.cummax(jnp.where(resets > 0, seg_index, 0), axis=0)
    position = seg_index - last_start
    cut = (resets == 0) & (position % truncation_segments[0] == 0)
    carried = jnp.where((resets > 0) | cut, 0, 1)
    pair = jnp.stack([resets[mp], carried[mp]]).astype(F32)
    flags = jnp.broadcast_to(jnp.pad(pair, (0, 6))[:, None], (8, 128))
    valid = lax.dynamic_slice_in_dim(key_mask, mp * SEG, SEG, 0)
    valid = jnp.concatenate([valid, jnp.ones((MEM,), jnp.int32), jnp.zeros((PAD - MEM,), jnp.int32)])
    kbias = jnp.where(valid > 0, 0.0, -1e30).astype(F32)[None, :]

    lo, dx, dqkv, dot_w, dup, ddnt, dmem, dnorm = run_layer(
        n, tokens, cotangent, flags, kbias, norms, mem_init, block[:3], block[3], wup, wdnt
    )
    dblock = jnp.concatenate([dqkv, dot_w[None]], axis=0)
    dblock = dblock.reshape(4, m, rows, n, cols).transpose(3, 1, 0, 2, 4).reshape(n * m, 4, rows, cols)
    dblock = lax.psum_scatter(dblock, ("mp", "dp"), scatter_dimension=0).astype(F32)
    dup = lax.psum_scatter(
        dup.reshape(n * m, rows, -1), ("mp", "dp"), scatter_dimension=0
    ).astype(F32)
    ddnt = lax.psum_scatter(
        ddnt.reshape(n * m, rows, -1), ("mp", "dp"), scatter_dimension=0
    ).astype(F32)
    tiny = lax.psum(jnp.concatenate([dmem[:MEM], dnorm[:4]], axis=0), ("mp", "dp"))
    tiny = lax.dynamic_slice_in_dim(tiny, dp * rows, rows, 1)
    return (
        lo,
        dx.astype(F32).reshape(n * SEG, cols),
        dblock[:3],
        dblock[3].T,
        dup,
        ddnt.T,
        tiny[:MEM],
        tiny[MEM],
        tiny[MEM + 1],
        tiny[MEM + 2],
        tiny[MEM + 3],
    )


def solution(mesh):
    return jax.shard_map(
        shards,
        mesh=mesh,
        in_specs=(
            P("dp", None), P("dp", None), P("dp"), P("dp"), P(),
            P(None, "dp", "mp"), P("mp", "dp"), P("dp", "mp"), P("mp", "dp"), P(None, "dp"),
            P("dp"), P("dp"), P("dp"), P("dp"),
        ),
        out_specs=(
            P("dp", None), P("dp", "mp"), P(None, "dp", "mp"), P("mp", "dp"), P("dp", "mp"),
            P("mp", "dp"), P(None, "dp"), P("dp"), P("dp"), P("dp"), P("dp"),
        ),
        check_vma=False,
    )
```

time: 1480 us -> 895 us (0.60)
  blocking collectives: 801 us -> 10.6 us
  waiting for transfers between devices: 201 us -> 586 us
  Pallas kernels: 0 us -> 198 us
  matrix products: 169 us -> 0 us
  local copies, waits for them, and re-layouts: 146 us -> 60.1 us
  other arithmetic: 87.4 us -> 19.3 us
  starting transfers between devices: 27.1 us -> 0.28 us
  loops' own time: 17.4 us -> 0 us
    all_gather x23 -> x1, blocking collectives: 352 us -> 10.6 us  [shards(): small = lax.all_gather(small, 'dp', axis=1, tiled=True)]
    while x12 -> x0, blocking collectives: 332 us -> none
    reduce_scatter x3, waiting for transfers between devices: 138 us -> 339 us  [the longest x1 119 us: shards(): lax.psum_scatter(dblock, ('mp', 'dp'), scatter_dimension=0).astype(F32)]
    pallas_call x0 -> x1, Pallas kernels: none -> 198 us  [run_layer(): pl.pallas_call(functools.partial(layer_kernel, n), out_shape=out_shape, i...]
    dot_general x72 -> x0, matrix products: 166 us -> none  [the longest x12 32.9 us: contract_rows(): jnp.einsum('ri,rj->ij', left, right, preferred_element_type=jnp.float32)]
    all_gather x2 -> x3, waiting for transfers between devices: 0.01 us -> 156 us  [the longest x1 65.4 us: shards(): lax.all_gather(down_weight.T, ('mp', 'dp'), axis=0).reshape(n, width, -1)]
    psum x0 -> x1, waiting for transfers between devices: none -> 88.6 us  [shards(): lax.psum(jnp.concatenate([dmem[:MEM], dnorm[:4]], axis=0), ('mp', 'dp'))]
    psum x5 -> x0, blocking collectives: 78.9 us -> none  [the longest x4 69.1 us: from_root(): return lax.psum(kept, axis)]
  transfers between devices with their start and end apart: 23 -> 7, of which waited for: 8 -> 7; matrix products, arithmetic and copies ran while one was open for 10% -> 8% of each run, Pallas kernels for 0% -> 0%
where the time goes in v1:
time: 895 us; the launch traced here: 890 us
  waiting for transfers between devices  586 us (65%)
  Pallas kernels  198 us (22%)
  local copies, waits for them, and re-layouts  60.1 us (7%)
  other arithmetic  19.3 us (2%)
  between operations  15.1 us (2%)
  blocking collectives  10.6 us (1%)
    pallas_call x1, Pallas kernels, run_layer(): pl.pallas_call(functools.partial(layer_kernel, n), out_shape=out_shape, i...  198 us
    reduce_scatter x1, waiting for transfers between devices, shards(): lax.psum_scatter(dblock, ('mp', 'dp'), scatter_dimension=0).astype(F32)  119 us
    reduce_scatter x1, waiting for transfers between devices, shards(): lax.psum_scatter(dup.reshape(n * m, rows, -1), ('mp', 'dp'), scatter_dime...  111 us
    reduce_scatter x1, waiting for transfers between devices, shards(): lax.psum_scatter(ddnt.reshape(n * m, rows, -1), ('mp', 'dp'), scatter_dim...  109 us
    psum x1, waiting for transfers between devices, shards(): lax.psum(jnp.concatenate([dmem[:MEM], dnorm[:4]], axis=0), ('mp', 'dp'))  88.6 us
    all_gather x1, waiting for transfers between devices, shards(): lax.all_gather(down_weight.T, ('mp', 'dp'), axis=0).reshape(n, width, -1)  65.4 us
    all_gather x1, waiting for transfers between devices, shards(): block = lax.all_gather(block, ('mp', 'dp'), axis=0)  51.3 us
    all_gather x1, waiting for transfers between devices, shards(): wup = lax.all_gather(up_weight, ('mp', 'dp'), axis=0).reshape(n, width, -1)  39.1 us
  transfers between devices with their start and end apart: 7, of which 7 were waited for; matrix products, arithmetic and copies ran while one was open for 8% of the time, Pallas kernels for 0%

profile of v1, /device:TPU:0, one launch (start us, length us, event | category | flops | bytes accessed | tf_op | source)
XLA Modules:
  0.0 889.7 jit_solution(14484751634973522516)
XLA Ops:
  8.1 1.6 pad_maximum_fusion
  15.5 1.5 concatenate.37
  17.0 10.6 %all-gather.3 = bf16[8,96,24]{1,2,0:T(8,128)(2,1)S(1)} all-gather(bf16[1,96,24]{1,2,0:T(8,128)(2,1)S(1)} %bitcast.72), channel_id=1, replica_groups=mesh['dp'=8,'mp'=4] {'dp'}, dimensions={0}, use_global_device_ids=true | all-gather | bytes 41472 | tf_op jit(solution)/shard_map/all_gather | solution.py:429
  32.5 51.3 %all-gather.8.cloned.1.call-done = bf16[128,96,192]{2,1,0:T(8,128)(2,1)} async-done(((bf16[4,96,192]{2,1,0:T(8,128)(2,1)}), bf16[128,96,192]{2,1,0:T(8,128)(2,1)}) %all-gather.8.cloned.1.call-update) | async-done | bytes 4718608 | tf_op jit(solution)/shard_map/all_gather | solution.py:421
  83.7 8.7 copy.43
  92.4 4.3 slice.65
  96.7 1.7 slice.66
  98.5 9.0 %slice.51.wqkv_hbm = bf16[3,768,768]{2,1,0:T(8,128)(2,1)} reshape(bf16[3,8,96,4,192]{4,3,2,1,0:T(4,128)(2,1)} %slice.65) | data formatting | bytes 7077888 | tf_op jit(solution)/shard_map/slice | solution.py:444
  107.5 2.2 squeeze.22.wot_hbm
  109.7 39.1 %all-gather.10.cloned.1.call-done = bf16[3072,768]{1,0:T(8,128)(2,1)} async-done(((bf16[96,768]{1,0:T(8,128)(2,1)}), bf16[3072,768]{1,0:T(8,128)(2,1)}) %all-gather.10.cloned.1.call-update) | async-done | bytes 4718608 | tf_op jit(solution)/shard_map/all_gather | solution.py:423
  148.8 65.4 %all-gather.12.cloned.1.call-done = bf16[3072,768]{1,0:T(8,128)(2,1)} async-done(((bf16[96,768]{1,0:T(8,128)(2,1)}), bf16[3072,768]{1,0:T(8,128)(2,1)}) %all-gather.12.cloned.1.call-update) | async-done | bytes 4718608 | tf_op jit(solution)/shard_map/all_gather | solution.py:424
  214.9 198.3 %shard_map.221 = (bf16[2048,768]{1,0:T(8,128)(2,1)}, bf16[4,512,192]{2,1,0:T(8,128)(2,1)}, bf16[3,768,768]{2,1,0:T(8,128)(2,1)}, bf16[768,768]{1,0:T(8,128)(2,1)...) custom-call(bf16[2048,768]{1,0:T(8,128)(2,1)} %tok_hbm.1, ...), custom_call_target="tpu_custom_call" | custom-call | flops 25999998976 | bytes 40000000 | tf_op jit(solution)/shard_map/pallas_call | solution.py:382
  415.6 10.1 %concatenate.39 = bf16[3,8,96,4,192]{4,3,2,1,0:T(4,128)(2,1)} reshape(bf16[3,768,768]{2,1,0:T(8,128)(2,1)} %get-tuple-element.21) | data formatting | bytes 7077888 | tf_op jit(solution)/shard_map/concatenate | solution.py:446
  425.7 2.3 concatenate.40
  428.0 7.6 maximum_bitcast_fusion
  435.6 3.8 copy.39
  441.0 1.7 copy.40
  442.7 88.6 %all-reduce.4.cloned.1.call-done = f32[24,768]{1,0:T(8,128)} async-done(((f32[24,768]{1,0:T(8,128)}), f32[24,768]{1,0:T(8,128)}) %all-reduce.4.cloned.1.call-update) | async-done | bytes 73744 | tf_op jit(solution)/shard_map/psum | solution.py:455
  534.1 119.0 %reduce-scatter.4.cloned.1.call-done = bf16[1,4,96,192]{3,2,1,0:T(8,128)(2,1)} async-done(((bf16[32,4,96,192]{3,2,1,0:T(8,128)(2,1)}), bf16[1,4,96,192]{3,2,1,0:T(8,128)(2,1)}) %reduce-scatter.4.cloned.1.call-update) | async-done | bytes 147472 | tf_op jit(solution)/shard_map/reduce_scatter | solution.py:448
  654.9 110.8 %reduce-scatter.6.cloned.1.call-done = bf16[1,96,768]{2,1,0:T(8,128)(2,1)} async-done(((bf16[32,96,768]{2,1,0:T(8,128)(2,1)}), bf16[1,96,768]{2,1,0:T(8,128)(2,1)}) %reduce-scatter.6.cloned.1.call-update) | async-done | bytes 147472 | tf_op jit(solution)/shard_map/reduce_scatter | solution.py:449
  765.6 1.6 bitcast_convert_fusion.1
  768.0 109.2 %reduce-scatter.8.cloned.1.call-done = bf16[1,96,768]{2,1,0:T(8,128)(2,1)} async-done(((bf16[32,96,768]{2,1,0:T(8,128)(2,1)}), bf16[1,96,768]{2,1,0:T(8,128)(2,1)}) %reduce-scatter.8.cloned.1.call-update) | async-done | bytes 147472 | tf_op jit(solution)/shard_map/reduce_scatter | solution.py:452
  877.2 1.6 convert_bitcast_fusion
  878.9 3.8 copy.47
  (50 shorter events, 20.7 us)
Async XLA Ops:
  7.2 76.6 %all-gather.8.cloned.1.call-start = ((), (), s32[]{:S(2)}) async-start(), calls=%async_computation.7 | async-start | bytes 6488064 | tf_op jit(solution)/shard_map/all_gather | solution.py:421
  9.8 139.1 %all-gather.10.cloned.1.call-start = ((), (), s32[]{:S(2)}) async-start(), calls=%async_computation.8 | async-start | bytes 4866048 | tf_op jit(solution)/shard_map/all_gather | solution.py:423
  10.5 203.7 %all-gather.12.cloned.1.call-start = ((), (), s32[]{:S(2)}) async-start(), calls=%async_computation.9 | async-start | bytes 4866048 | tf_op jit(solution)/shard_map/all_gather | solution.py:424
  11.3 520.0 %all-reduce.4.cloned.1.call-start = ((), (), s32[]{:S(2)}) async-start(), calls=%async_computation.6 | async-start | bytes 147456 | tf_op jit(solution)/shard_map/psum | solution.py:455
  98.5 9.0 %copy-start = (bf16[1,8,96,4,192]{4,3,2,1,0:T(4,128)(2,1)S(1)}, bf16[1,8,96,4,192]{4,3,2,1,0:T(4,128)(2,1)}, u32[]{:S(2)}) copy-start(bf16[1,8,96,4,192]{4,3,2,1,0:T(4,128)(2,1)} %slice.66) | copy-start | bytes 3538948
  413.2 12.6 %copy-start.1 = (bf16[768,768]{1,0:T(8,128)(2,1)S(1)}, bf16[768,768]{1,0:T(8,128)(2,1)}, u32[]{:S(2)}) copy-start(bf16[768,768]{1,0:T(8,128)(2,1)} %get-tuple-element.22) | copy-start | bytes 3538948
  415.6 237.6 %reduce-scatter.4.cloned.1.call-start = ((), (), s32[]{:S(2)}) async-start(), calls=%async_computation.3 | async-start | bytes 6488064 | tf_op jit(solution)/shard_map/reduce_scatter | solution.py:448
  439.4 326.2 %reduce-scatter.6.cloned.1.call-start = ((), (), s32[]{:S(2)}) async-start(), calls=%async_computation.4 | async-start | bytes 4866048 | tf_op jit(solution)/shard_map/reduce_scatter | solution.py:449
  439.5 1.3 copy-start.2
  440.0 437.3 %reduce-scatter.8.cloned.1.call-start = ((), (), s32[]{:S(2)}) async-start(), calls=%async_computation.5 | async-start | bytes 4866048 | tf_op jit(solution)/shard_map/reduce_scatter | solution.py:452
Sparse Core Ops, SparseCore 0:
  11.4 72.2 all-gather.7
  86.6 62.1 all-gather.9
  151.7 62.4 all-gather.11
  415.7 115.5 all-reduce.3
  536.8 116.3 reduce-scatter.3
  659.4 106.1 reduce-scatter.5
  771.1 106.0 reduce-scatter.7
